TPU v7x, 512 devices: a whole 4x4x16 slice. The times are simulated.
512 devices in a mesh: dp: 64 (over z, x_hi, core), layer: 8 (over x_lo, y).
Axes of the slice: x: 4 (x_hi: 2, x_lo: 2; x = x_hi * 2 + x_lo), y: 4, z: 16, core: 2. Of those that a mesh axis runs over, the one named last changes fastest.
Arguments:
- train_grads: bfloat16 [16384, 8, 4096], P('dp', 'layer'), may hold values from -6 to 6
- query_grads: bfloat16 [4, 512, 8, 4096], P(None, 'dp', 'layer'), may hold values from -6 to 6
- out_basis: float32 [8, 64, 64], P('layer'), may hold values from -0.75 to 0.75
- in_basis: float32 [8, 64, 64], P('layer'), may hold values from -0.75 to 0.75
- eigenvalues: float32 [8, 4096], P('layer'), may hold values from 0.5 to 8
- block_order: int32 [4], replicated, may hold values from 0 to 3, each once
Outputs:
- scores: float32 [3, 512, 16384], P(None, 'layer', 'dp')
Inputs may be any that keep to these rules, and one draw needn't show every extreme that they name: `block_order`: a permutation of 0 to 3.
All inputs are finite; a program needn't handle non-finite values.
Results may differ from a plain program's by a relative error of at most 0.0029.
Values may be sent and summed in bfloat16 or wider, within the bound.
A program may use at most 64 MiB of HBM per device.

v0:
```python
import math

import jax
import jax.numpy as jnp
from jax import lax
from jax.sharding import PartitionSpec as P

STEPS = 3


def precondition(raw_rows, out_basis, in_basis, eigenvalues):
    row_total = raw_rows.shape[0]
    layer_count = raw_rows.shape[1]
    proj_width = raw_rows.shape[2]
    out_width = out_basis.shape[1]
    in_width = in_basis.shape[1]
    precise = lax.Precision.HIGHEST
    grid_form = raw_rows.astype(jnp.float32).reshape(row_total, layer_count, out_width, in_width)
    half_turn = jnp.einsum("qlab,lbd->qlad", grid_form, in_basis, precision=precise)
    rotated = jnp.einsum("qlad,lac->qlcd", half_turn, out_basis, precision=precise)
    scaled = rotated / eigenvalues.reshape(layer_count, out_width, in_width)
    back_half = jnp.einsum("qlcd,led->qlce", scaled, in_basis, precision=precise)
    result = jnp.einsum("qlce,lac->qlae", back_half, out_basis, precision=precise)
    return result.reshape(row_total, layer_count, proj_width).astype(jnp.bfloat16)


def body(train_grads, query_grads, out_basis, in_basis, eigenvalues, block_order):
    train_rows = train_grads.shape[0]
    lay_local = train_grads.shape[1]
    proj_width = train_grads.shape[2]
    factor = 1.0 / math.sqrt(lay_local * lax.axis_size("layer") * proj_width)
    train_flat = train_grads.reshape(train_rows, lay_local * proj_width)

    def ready_block(step_index):
        raw_rows = lax.dynamic_index_in_dim(query_grads, block_order[step_index], 0, keepdims=False)
        ready = precondition(raw_rows, out_basis, in_basis, eigenvalues)
        return ready.reshape(ready.shape[0], lay_local * proj_width)

    def score_rows(query_part):
        inner = query_part.ndim - 1
        product = lax.dot_general(
            query_part, train_flat, (((inner,), (1,)), ((), ())), preferred_element_type=jnp.float32
        )
        return product * factor

    partial_list = [
        score_rows(lax.all_gather(ready_block(step_index), "dp", axis=0, tiled=True))
        for step_index in range(STEPS)
    ]
    totals = jnp.stack(
        [
            lax.psum_scatter(partial_value, "layer", scatter_dimension=0, tiled=True)
            for partial_value in partial_list
        ]
    )
    return totals


def solution(mesh):
    placed = (
        P("dp", "layer", None),
        P(None, "dp", "layer", None),
        P("layer", None, None),
        P("layer", None, None),
        P("layer", None),
        P(),
    )
    return jax.shard_map(
        body, mesh=mesh, in_specs=placed, out_specs=P(None, "layer", "dp"), check_vma=False
    )
```

profile of v0, /device:TPU:6, one launch (start us, length us, event | category | flops | bytes accessed | tf_op | source)
XLA Modules:
  0.0 620.2 jit_solution(7165200070436545653)
XLA Ops:
  6.5 1.5 fusion.42
  11.9 0.5 broadcast.14
  12.4 1.3 reduce.3
  15.8 0.9 constant_dynamic-slice_fusion.2
  16.9 1.3 fusion.40
  18.1 1.1 fusion.19
  19.3 1.1 fusion.38
  20.4 1.1 fusion.15
  21.7 0.8 convert_element_type.61
  22.7 1.3 fusion.32
  25.2 0.8 convert_element_type.71
  26.3 0.5 fusion.36
  27.2 0.4 fusion.34
  28.1 0.8 convert_element_type.66
  29.0 147.6 %all-gather.4.cloned.1.call-done = bf16[512,4096]{1,0:T(8,128)(2,1)} async-done(((bf16[8,4096]{1,0:T(8,128)(2,1)}), bf16[512,4096]{1,0:T(8,128)(2,1)}) %all-gather.4.cloned.1.call-update) | async-done | bytes 4194320 | tf_op jit(solution)/shard_map/all_gather | solution.py:47
  176.6 4.3 fusion.6
  180.9 144.4 %all-gather.8.cloned.1.call-done = bf16[512,4096]{1,0:T(8,128)(2,1)} async-done(((bf16[8,4096]{1,0:T(8,128)(2,1)}), bf16[512,4096]{1,0:T(8,128)(2,1)}) %all-gather.8.cloned.1.call-update) | async-done | bytes 4194320 | tf_op jit(solution)/shard_map/all_gather | solution.py:47
  325.4 4.3 fusion.12
  329.7 144.5 %all-gather.6.cloned.1.call-done = bf16[512,4096]{1,0:T(8,128)(2,1)} async-done(((bf16[8,4096]{1,0:T(8,128)(2,1)}), bf16[512,4096]{1,0:T(8,128)(2,1)}) %all-gather.6.cloned.1.call-update) | async-done | bytes 4194320 | tf_op jit(solution)/shard_map/all_gather | solution.py:47
  474.2 4.3 fusion.9
  478.5 39.1 %reduce-scatter.4.cloned.1.call-done = f32[64,256]{1,0:T(8,128)} async-done(((f32[512,256]{1,0:T(8,128)}), f32[64,256]{1,0:T(8,128)}) %reduce-scatter.4.cloned.1.call-update) | async-done | bytes 65552 | tf_op jit(solution)/shard_map/reduce_scatter | solution.py:52
  517.6 47.2 %reduce-scatter.8.cloned.1.call-done = f32[64,256]{1,0:T(8,128)} async-done(((f32[512,256]{1,0:T(8,128)}), f32[64,256]{1,0:T(8,128)}) %reduce-scatter.8.cloned.1.call-update) | async-done | bytes 65552 | tf_op jit(solution)/shard_map/reduce_scatter | solution.py:52
  564.8 47.0 %reduce-scatter.6.cloned.1.call-done = f32[64,256]{1,0:T(8,128)} async-done(((f32[512,256]{1,0:T(8,128)}), f32[64,256]{1,0:T(8,128)}) %reduce-scatter.6.cloned.1.call-update) | async-done | bytes 65552 | tf_op jit(solution)/shard_map/reduce_scatter | solution.py:52
  611.8 1.6 pad_maximum_fusion
  (31 shorter events, 3.2 us)
Async XLA Ops:
  6.5 170.1 %copy-start = (bf16[256,1,4096]{2,0,1:T(8,128)(2,1)S(1)}, bf16[256,1,4096]{2,0,1:T(8,128)(2,1)}, u32[]{:S(2)}) copy-start(bf16[256,1,4096]{2,0,1:T(8,128)(2,1)} %param.6) | copy-start | bytes 6291460
  6.5 17.8 %copy-start.1 = (f32[1,64,64]{2,1,0:T(8,128)S(1)}, f32[1,64,64]{2,1,0:T(8,128)}, u32[]{:S(2)}) copy-start(f32[1,64,64]{2,1,0:T(8,128)} %param.9) | copy-start | bytes 49156
  6.5 17.5 %copy-start.2 = (f32[1,64,64]{2,1,0:T(8,128)S(1)}, f32[1,64,64]{2,1,0:T(8,128)}, u32[]{:S(2)}) copy-start(f32[1,64,64]{2,1,0:T(8,128)} %param.8) | copy-start | bytes 49156
  6.5 170.0 %all-gather.4.cloned.1.call-start = ((), (), s32[]{:S(2)}) async-start(), calls=%async_computation.3 | async-start | bytes 4259840 | tf_op jit(solution)/shard_map/all_gather | solution.py:47
  22.5 302.9 %all-gather.8.cloned.1.call-start = ((), (), s32[]{:S(2)}) async-start(), calls=%async_computation.7 | async-start | bytes 4259840 | tf_op jit(solution)/shard_map/all_gather | solution.py:47
  26.1 448.1 %all-gather.6.cloned.1.call-start = ((), (), s32[]{:S(2)}) async-start(), calls=%async_computation.5 | async-start | bytes 4259840 | tf_op jit(solution)/shard_map/all_gather | solution.py:47
  28.9 488.7 %reduce-scatter.4.cloned.1.call-start = ((), (), s32[]{:S(2)}) async-start(), calls=%async_computation.4 | async-start | bytes 589824 | tf_op jit(solution)/shard_map/reduce_scatter | solution.py:52
  180.9 383.9 %reduce-scatter.8.cloned.1.call-start = ((), (), s32[]{:S(2)}) async-start(), calls=%async_computation.8 | async-start | bytes 589824 | tf_op jit(solution)/shard_map/reduce_scatter | solution.py:52
  329.7 282.1 %reduce-scatter.6.cloned.1.call-start = ((), (), s32[]{:S(2)}) async-start(), calls=%async_computation.6 | async-start | bytes 589824 | tf_op jit(solution)/shard_map/reduce_scatter | solution.py:52
Sparse Core Ops, SparseCore 0:
  22.6 153.9 all-gather.3
  179.9 145.4 all-gather.7
  328.7 145.4 all-gather.5
  476.9 40.6 reduce-scatter.3
  520.5 44.2 reduce-scatter.7
  567.5 44.2 reduce-scatter.5
where the time goes:
time: 621 us; the launch traced here: 620 us
  waiting for transfers between devices  570 us (92%)
  matrix products  21.5 us (3%)
  between operations  19.3 us (3%)
  local copies, waits for them, and re-layouts  6.4 us (1%)
    all_gather x3, waiting for transfers between devices, body(): lax.all_gather(ready_block(step_index), 'dp', axis=0, tiled=True)  437 us
    reduce_scatter x3, waiting for transfers between devices, body(): lax.psum_scatter(partial_value, 'layer', scatter_dimension=0, tiled=True)  133 us
    dot_general x3, matrix products, score_rows(): lax.dot_general(query_part, train_flat, (((inner,), (1,)), ((), ())), pre...  12.9 us
  transfers between devices with their start and end apart: 6, of which 6 were waited for; matrix products, arithmetic and copies ran while one was open for 3% of the time, Pallas kernels for 0%

commit v1 on v0

v1 whole, which is shorter than its diff:
```python
import math

import jax
import jax.numpy as jnp
from jax import lax
from jax.experimental import pallas as pl
from jax.experimental.pallas import tpu as pltpu
from jax.sharding import PartitionSpec as P

STEPS = 3
MESH = pl.DeviceIdType.MESH
F32 = jnp.float32
BF16 = jnp.bfloat16
LATE = 5
CATCH = 6


def mm(a, b):
    return lax.dot_general(a, b, (((1,), (0,)), ((), ())), preferred_element_type=F32)


def split(x, parts):
    out = []
    for _ in range(parts):
        top = x.astype(BF16)
        out.append(top)
        x = x - top.astype(F32)
    return out


def mm3(x, y):
    return mm(x[0], y[0]) + (mm(x[0], y[1]) + mm(x[1], y[0]))


def twice(m):
    zero = jnp.zeros_like(m)
    return jnp.concatenate(
        [jnp.concatenate([m, zero], axis=1), jnp.concatenate([zero, m], axis=1)], axis=0
    )


def spread(m_parts):
    rows = lax.broadcasted_iota(jnp.int32, (512, 64), 0)
    cols = lax.broadcasted_iota(jnp.int32, (512, 64), 1)
    pick_row = ((rows // 256) + 2 * ((rows % 256) // 8) == cols).astype(F32).astype(BF16)
    k_rows = lax.broadcasted_iota(jnp.int32, (64, 512), 0)
    k_cols = lax.broadcasted_iota(jnp.int32, (64, 512), 1)
    pick_col = ((k_cols // 256) + 2 * ((k_cols % 256) // 8) == k_rows).astype(F32).astype(BF16)
    row_q = lax.broadcasted_iota(jnp.int32, (512, 512), 0) % 8
    col_q = lax.broadcasted_iota(jnp.int32, (512, 512), 1) % 8
    same = row_q == col_q
    out = []
    for part in m_parts:
        tall = mm(pick_row, part).astype(BF16)
        full = mm(tall, pick_col)
        out.append(jnp.where(same, full, 0.0).astype(BF16))
    return out


def left_apply(kron_parts, blocks):
    lane = lax.broadcasted_iota(jnp.int32, (256, 128), 1)
    low = lane < 64

    def turn(v):
        return pltpu.roll(v, 64, 1)

    b0, b1, b2 = blocks
    even = jnp.concatenate([jnp.where(low, b0, turn(b1)), b2], axis=1)
    odd = jnp.concatenate([jnp.where(low, turn(b0), b1), turn(b2)], axis=1)
    right = jnp.concatenate([even, odd], axis=0)
    out = mm3(kron_parts, split(right, 2))
    top, bot = out[:256], out[256:]
    r0 = jnp.where(low, top[:, :128], turn(bot[:, :128]))
    r1 = jnp.where(low, turn(top[:, :128]), bot[:, :128])
    r2 = jnp.where(low, top[:, 128:], turn(bot[:, 128:]))
    return r0, r1, r2


def stack_groups(x, count):
    return jnp.concatenate([x[:, g * 128 : (g + 1) * 128] for g in range(count)], axis=0)


def unstack_groups(x, first, count):
    return jnp.concatenate([x[(first + g) * 8 : (first + g + 1) * 8] for g in range(count)], axis=1)


def kernel(
    order_ref, train_ref, query_ref, a_ref, b_ref, lam_ref, out_ref,
    tbuf, qbuf, pf, xqs, xqr, own, ysend, ybuf, xsend, xbuf,
    train_sem, xq_ssem, xq_rsem, zs_ssem, c_ssem, z_rsem, c_rsem, y_ssem, y_rsem, x_ssem, x_rsem,
):
    dp = lax.axis_index("dp")
    layer = lax.axis_index("layer")
    z, h, c = dp // 4, (dp // 2) % 2, dp % 2
    lx, y = layer // 4, layer % 4
    x = 2 * h + lx

    def at(zz, hh, cc, ll, yy):
        return (4 * zz + 2 * hh + cc, 4 * ll + yy)

    def at_x(xx):
        return at(z, xx // 2, c, xx % 2, y)

    right, left = at((z + 1) % 16, h, c, lx, y), at((z + 15) % 16, h, c, lx, y)
    other_core = at(z, h, 1 - c, lx, y)
    partner = at(z, 1 - h, c, lx, y)
    y_peers = [at(z, h, c, lx, (y + k) % 4) for k in (1, 2, 3)]
    x_peers = [at_x((x + k) % 4) for k in (1, 2, 3)]

    barrier = pltpu.get_barrier_semaphore()
    everyone = [right, left, other_core] + y_peers + x_peers
    for device in everyone:
        pl.semaphore_signal(barrier, inc=1, device_id=device, device_id_type=MESH)

    def remote(src, dst, ssem, rsem, device):
        return pltpu.make_async_remote_copy(
            src_ref=src, dst_ref=dst, send_sem=ssem, recv_sem=rsem, device_id=device, device_id_type=MESH
        )

    half = 2048
    local_train = pltpu.make_async_copy(
        train_ref.at[:, pl.ds(pl.multiple_of(h * half, half), half)], tbuf.at[h], train_sem.at[0]
    )
    local_train.start()

    b_mat = b_ref[0]
    a_mat = a_ref[0]
    forth = split(twice(b_mat), 3)
    back = split(twice(b_mat.T), 2)
    a_parts = split(a_mat, 2)
    at_parts = split(a_mat.T, 2)
    kron_in = spread(at_parts)
    kron_out = spread(a_parts)
    lam = lam_ref[...]
    lam_rows = jnp.concatenate(
        [jnp.broadcast_to(lam[:, g * 128 : (g + 1) * 128], (8, 128)) for g in range(32)], axis=0
    )
    first = []
    for s in range(STEPS):
        raw = stack_groups(query_ref[order_ref[s]].astype(F32), 32).astype(BF16)
        first.append(mm(raw, forth[0]) + (mm(raw, forth[1]) + mm(raw, forth[2])))
    rotated = left_apply(kron_in, first)
    scaled = [mm3(split(r / lam_rows, 2), back) for r in rotated]
    ready = left_apply(kron_out, scaled)
    for s in range(STEPS):
        pf[s, 0] = ready[s][:128]
        pf[s, 1] = ready[s][128:]

    pl.semaphore_wait(barrier, len(everyone))

    def xq(s):
        return remote(xqs.at[s], xqr.at[s], xq_ssem.at[s], xq_rsem.at[s], partner)

    for s in range(STEPS):
        away = pf[s, 1 - h]
        xqs[s] = jnp.concatenate(
            [unstack_groups(away, 0, 8), unstack_groups(away, 8, 8)], axis=0
        ).astype(BF16)
        xq(s).start()
    send_train = remote(
        train_ref.at[:, pl.ds(pl.multiple_of((1 - h) * half, half), half)],
        tbuf.at[h], train_sem.at[1], train_sem.at[2], partner,
    )
    send_train.start()

    def ring(zs, s, way, t):
        slot = qbuf.at[zs, c, s]
        return remote(slot, slot, zs_ssem.at[way, t, s], z_rsem.at[zs, s], right if way == 0 else left)

    def hand(zs, s):
        slot = qbuf.at[zs, c, s]
        return remote(slot, slot, c_ssem.at[zs, s], c_rsem.at[zs, s], other_core)

    def handed(zs, s):
        slot = qbuf.at[zs, 1 - c, s]
        return remote(slot, slot, c_ssem.at[zs, s], c_rsem.at[zs, s], other_core)

    for s in range(STEPS):
        here = unstack_groups(pf[s, h], 0, 16)
        xq(s).wait_recv()
        got = xqr[s].astype(F32)
        there = jnp.concatenate([got[:8], got[8:]], axis=1)
        slot = jnp.where(
            h == 0, jnp.concatenate([here, there], axis=0), jnp.concatenate([there, here], axis=0)
        )
        qbuf[z, c, s] = slot.astype(BF16)
        ring(z, s, 0, 0).start()
        ring(z, s, 1, 0).start()
        hand(z, s).start()

    def chunk(m):
        return (z + 16 + (1 - 2 * (m % 2)) * ((m + 1) // 2)) % 16

    def y_copy(zs, e):
        k = zs % 2 + 2 * (zs // 8)
        to = (zs // 2) % 4
        return remote(
            ysend.at[zs, e], ybuf.at[k, y, e], y_ssem.at[zs, e], y_rsem.at[k, y, e], at(z, h, c, lx, to)
        )

    def score(m, e, fresh):
        zs = chunk(m)
        if fresh:
            for s in range(STEPS):
                handed(zs, s).wait_recv()
        lhs = qbuf[zs].reshape(96, half)
        part = lax.dot_general(lhs, tbuf[e], (((1,), (1,)), ((), ())), preferred_element_type=F32)
        k = zs % 2 + 2 * (zs // 8)

        @pl.when((zs // 2) % 4 == y)
        def _():
            own[k, e] = part

        @pl.when((zs // 2) % 4 != y)
        def _():
            ysend[zs, e] = part.astype(BF16)
            y_copy(zs, e).start()

    def x_copy(zs, e):
        k = zs % 2 + 2 * (zs // 8)
        return remote(
            xsend.at[k, e], xbuf.at[zs % 2, x], x_ssem.at[k, e], x_rsem.at[zs % 2, x],
            at(z, e, c, zs // 8, y),
        )

    def join(m, e):
        zs = chunk(m)
        k = zs % 2 + 2 * (zs // 8)

        @pl.when((zs // 2) % 4 == y)
        def _():
            total = own[k, e]
            for step in (1, 2, 3):
                src = (y + step) % 4
                slot = ybuf.at[k, src, e]
                remote(slot, slot, y_ssem.at[zs, e], y_rsem.at[k, src, e], right).wait_recv()
                total = total + ybuf[k, src, e].astype(F32)
            mine = 2 * e + zs // 8 == x

            @pl.when(mine)
            def _():
                xbuf[zs % 2, x] = total

            @pl.when(jnp.logical_not(mine))
            def _():
                xsend[k, e] = total
                x_copy(zs, e).start()

    def over(lo, hi, f):
        if hi > lo:

            @pl.loop(lo, hi)
            def _(m):
                f(m)

    waiting = []
    caught = 0
    for t in range(1, 9):
        for s in range(STEPS):
            if t < 8:
                for way in (0, 1):
                    zs = (z + 16 - t) % 16 if way == 0 else (z + t) % 16
                    ring(zs, s, way, t).wait_recv()
                    if t < 7 or (way == 0 and s == 0) or (way == 1 and s == 2):
                        ring(zs, s, way, t).start()
                    elif s == 1:

                        @pl.when(c == way)
                        def _():
                            ring(zs, s, way, t).start()

                    hand(zs, s).start()
            else:
                zs = (z + 8) % 16
                ring(zs, s, 0, 0).wait_recv()
                hand(zs, s).start()
        if t == 1:
            local_train.wait()
        lo, hi = max(2 * t - 3, 0), 2 * t - 1
        over(lo, hi, lambda m: score(m, h, True))
        done = [(lo, hi, True)]
        if t >= LATE:
            if t == LATE:
                local = tbuf.at[1 - h]
                remote(local, local, train_sem.at[1], train_sem.at[2], partner).wait_recv()
            top = min(caught + CATCH, hi)
            over(caught, top, lambda m: score(m, 1 - h, False))
            done.append((caught, top, False))
            caught = top
        for lo, hi, mine in waiting:
            over(lo, hi, lambda m: join(m, h if mine else 1 - h))
        waiting = done
    score(15, h, True)
    score(15, 1 - h, False)
    for lo, hi, mine in waiting + [(15, 16, True), (15, 16, False)]:
        over(lo, hi, lambda m: join(m, h if mine else 1 - h))

    factor = 1.0 / math.sqrt(8 * 4096)
    for j in (0, 1):
        total = xbuf[j, x]
        for step in (1, 2, 3):
            src = (x + step) % 4
            slot = xbuf.at[j, src]
            remote(slot, slot, x_ssem.at[0, 0], x_rsem.at[j, src], right).wait_recv()
            total = total + xbuf[j, src]
        total = total * factor
        for cc in range(2):
            for s in range(STEPS):
                for hh in range(2):
                    row = cc * 48 + s * 16 + hh * 8
                    to = 32 * j + 16 * hh + 8 * cc
                    out_ref[s, to : to + 8, :] = total[row : row + 8]

    send_train.wait_send()
    for s in range(STEPS):
        xq(s).wait_send()
        for t in range(8):
            for way in (0, 1):
                zs = (z + 16 - t) % 16 if way == 0 else (z + t) % 16
                if t < 7 or (way == 0 and s == 0) or (way == 1 and s == 2):
                    ring(zs, s, way, t).wait_send()
                elif s == 1:

                    @pl.when(c == way)
                    def _():
                        ring(zs, s, way, t).wait_send()

    @pl.loop(0, 16)
    def _(zs):
        for s in range(STEPS):
            hand(zs, s).wait_send()
        for e in (0, 1):

            @pl.when((zs // 2) % 4 != y)
            def _():
                y_copy(zs, e).wait_send()

            @pl.when(((zs // 2) % 4 == y) & (2 * e + zs // 8 != x))
            def _():
                x_copy(zs, e).wait_send()


def body(train_grads, query_grads, out_basis, in_basis, eigenvalues, block_order):
    train = train_grads.reshape(256, 4096)
    query = query_grads.reshape(4, 8, 4096)
    vmem = pl.BlockSpec(memory_space=pltpu.VMEM)
    dma = pltpu.SemaphoreType.DMA
    return pl.pallas_call(
        kernel,
        out_shape=jax.ShapeDtypeStruct((STEPS, 64, 256), F32),
        in_specs=[
            pl.BlockSpec(memory_space=pltpu.SMEM),
            pl.BlockSpec(memory_space=pl.ANY),
            vmem, vmem, vmem, vmem,
        ],
        out_specs=vmem,
        scratch_shapes=[
            pltpu.VMEM((2, 256, 2048), BF16),
            pltpu.VMEM((16, 2, 3, 16, 2048), BF16),
            pltpu.VMEM((3, 2, 128, 128), F32),
            pltpu.VMEM((3, 16, 1024), BF16),
            pltpu.VMEM((3, 16, 1024), BF16),
            pltpu.VMEM((4, 2, 96, 256), F32),
            pltpu.VMEM((16, 2, 96, 256), BF16),
            pltpu.VMEM((4, 4, 2, 96, 256), BF16),
            pltpu.VMEM((4, 2, 96, 256), F32),
            pltpu.VMEM((2, 4, 96, 256), F32),
            dma((3,)), dma((3,)), dma((3,)),
            dma((2, 8, 3)), dma((16, 3)), dma((16, 3)), dma((16, 3)),
            dma((16, 2)), dma((4, 4, 2)), dma((4, 2)), dma((2, 4)),
        ],
        compiler_params=pltpu.CompilerParams(
            collective_id=0, has_side_effects=True, vmem_limit_bytes=48 << 20
        ),
    )(block_order, train, query, out_basis, in_basis, eigenvalues)


def solution(mesh):
    placed = (
        P("dp", "layer", None),
        P(None, "dp", "layer", None),
        P("layer", None, None),
        P("layer", None, None),
        P("layer", None),
        P(),
    )
    return jax.shard_map(
        body, mesh=mesh, in_specs=placed, out_specs=P(None, "layer", "dp"), check_vma=False
    )
```

time: 621 us -> 84.4 us (0.14)
  the two profiles are of different devices: /device:TPU:6 before, /device:TPU:38 now
where the time goes in v1:
time: 84.4 us; the launch traced here: 84 us
  Pallas kernels  77.9 us (92%)
  local copies, waits for them, and re-layouts  6.11 us (7%)
    pallas_call x1, Pallas kernels, body(): pl.pallas_call(kernel, out_shape=jax.ShapeDtypeStruct((STEPS, 64, 256), F...  77.9 us
    unnamed x13, local copies, waits for them, and re-layouts  6.11 us

profile of v1, /device:TPU:38, one launch (start us, length us, event | category | flops | bytes accessed | tf_op | source)
XLA Modules:
  0.0 84.0 jit_solution(7151332056750578845)
XLA Ops:
  0.0 0.0 copy-start
  0.0 1.6 %copy-done = bf16[256,1,4096]{2,0,1:T(8,128)(2,1)S(1)} copy-done((bf16[256,1,4096]{2,0,1:T(8,128)(2,1)S(1)}, bf16[256,1,4096]{2,0,1:T(8,128)(2,1)}, u32[]{:S(2)}) %copy-start) | copy-done | bytes 2097176
  1.6 0.0 copy-start.1
  1.6 0.9 %copy-done.1 = bf16[4,8,1,4096]{3,1,2,0:T(8,128)(2,1)S(1)} copy-done((bf16[4,8,1,4096]{3,1,2,0:T(8,128)(2,1)S(1)}, bf16[4,8,1,4096]{3,1,2,0:T(8,128)(2,1)}, u32[]{:S(2)}) %copy-start.1) | copy-done | bytes 262168
  2.5 0.0 copy-start.2
  2.5 0.8 copy-done.2
  3.3 0.0 copy-start.3
  3.3 0.8 copy-done.3
  4.1 0.0 copy-start.4
  4.1 0.7 copy-done.4
  4.8 0.0 copy-start.5
  4.8 0.7 copy-done.5
  5.4 77.9 %shard_map.64 = f32[3,64,256]{2,1,0:T(8,128)S(1)} custom-call(s32[4]{0:T(128)S(1)} %copy-done.5, bf16[256,4096]{1,0:T(8,128)(2,1)S(1)} %bitcast.2, bf16[4,8,4096]{2,1,0:T(8,128)(2,1)S(1)} %bitcast.3, f32[1,64,64]{2,1,0:T(8,128)S(1)} %copy-done.2, f32[1,64,64]{2,1,0:T(8,128)S(1)} %copy-done.3, f32[1,4096]{1,0:T(1,128)S(1)} %copy-done.4), custom_call_target="tpu_custom_call" | custom-call | tf_op jit(solution)/shard_map/pallas_call | solution.py:348
  83.3 0.7 copy.8
Async XLA Ops:
  0.0 1.6 %copy-start = (bf16[256,1,4096]{2,0,1:T(8,128)(2,1)S(1)}, bf16[256,1,4096]{2,0,1:T(8,128)(2,1)}, u32[]{:S(2)}) copy-start(bf16[256,1,4096]{2,0,1:T(8,128)(2,1)} %param.6) | copy-start | bytes 6291460
  1.6 0.9 %copy-start.1 = (bf16[4,8,1,4096]{3,1,2,0:T(8,128)(2,1)S(1)}, bf16[4,8,1,4096]{3,1,2,0:T(8,128)(2,1)}, u32[]{:S(2)}) copy-start(bf16[4,8,1,4096]{3,1,2,0:T(8,128)(2,1)} %param.7) | copy-start | bytes 786436
  2.5 0.8 copy-start.2
  3.3 0.8 copy-start.3
  4.1 0.7 copy-start.4
  4.8 0.7 copy-start.5

commit v2 on v1

--- a/solution.py
+++ b/solution.py
@@ -11,6 +11,8 @@
 MESH = pl.DeviceIdType.MESH
 F32 = jnp.float32
 BF16 = jnp.bfloat16
+LAG_Y = 2
+LAG_X = 2
 LATE = 5
 CATCH = 6
 
@@ -85,9 +87,9 @@
 
 
 def kernel(
-    order_ref, train_ref, query_ref, a_ref, b_ref, lam_ref, out_ref,
-    tbuf, qbuf, pf, xqs, xqr, own, ysend, ybuf, xsend, xbuf,
-    train_sem, xq_ssem, xq_rsem, zs_ssem, c_ssem, z_rsem, c_rsem, y_ssem, y_rsem, x_ssem, x_rsem,
+    order_hbm, train_ref, query_hbm, a_hbm, b_hbm, lam_hbm, out_ref,
+    order_ref, query_ref, a_ref, b_ref, lam_ref, in_sem, tbuf, qbuf, pf, xqs, xqr, own, ysend, ybuf, xsend, xbuf, fsend, fbuf,
+    train_sem, xq_ssem, xq_rsem, zs_ssem, c_ssem, z_rsem, c_rsem, y_ssem, y_rsem, x_ssem, x_rsem, f_ssem, f_rsem,
 ):
     dp = lax.axis_index("dp")
     layer = lax.axis_index("layer")
@@ -98,17 +100,30 @@
     def at(zz, hh, cc, ll, yy):
         return (4 * zz + 2 * hh + cc, 4 * ll + yy)
 
+    copies = [
+        pltpu.make_async_copy(src, dst, in_sem.at[i])
+        for i, (src, dst) in enumerate(
+            [
+                (a_hbm, a_ref), (b_hbm, b_ref), (query_hbm, query_ref),
+                (order_hbm, order_ref), (lam_hbm, lam_ref),
+            ]
+        )
+    ]
+    for copy in copies:
+        copy.start()
+
     def at_x(xx):
         return at(z, xx // 2, c, xx % 2, y)
 
     right, left = at((z + 1) % 16, h, c, lx, y), at((z + 15) % 16, h, c, lx, y)
     other_core = at(z, h, 1 - c, lx, y)
     partner = at(z, 1 - h, c, lx, y)
-    y_peers = [at(z, h, c, lx, (y + k) % 4) for k in (1, 2, 3)]
-    x_peers = [at_x((x + k) % 4) for k in (1, 2, 3)]
 
     barrier = pltpu.get_barrier_semaphore()
-    everyone = [right, left, other_core] + y_peers + x_peers
+    everyone = [right, left, other_core]
+    for step in (1, 2, 3):
+        aside = (y + step) % 4
+        everyone += [at(z, h, c, lx, aside), at(z, h, c, 1 - lx, aside), at_x((x + step) % 4)]
     for device in everyone:
         pl.semaphore_signal(barrier, inc=1, device_id=device, device_id_type=MESH)
 
@@ -123,6 +138,8 @@
     )
     local_train.start()
 
+    copies[0].wait()
+    copies[1].wait()
     b_mat = b_ref[0]
     a_mat = a_ref[0]
     forth = split(twice(b_mat), 3)
@@ -131,6 +148,8 @@
     at_parts = split(a_mat.T, 2)
     kron_in = spread(at_parts)
     kron_out = spread(a_parts)
+    for copy in copies[2:]:
+        copy.wait()
     lam = lam_ref[...]
     lam_rows = jnp.concatenate(
         [jnp.broadcast_to(lam[:, g * 128 : (g + 1) * 128], (8, 128)) for g in range(32)], axis=0
@@ -191,11 +210,14 @@
     def chunk(m):
         return (z + 16 + (1 - 2 * (m % 2)) * ((m + 1) // 2)) % 16
 
-    def y_copy(zs, e):
-        k = zs % 2 + 2 * (zs // 8)
-        to = (zs // 2) % 4
+    def owner(m, cs, e):
+        return 2 * (e if isinstance(m, int) and m in (0, 15) else m % 2) + cs
+
+    def y_copy(m, cs, e):
+        zs, t, to = chunk(m), (m + 1) // 2, owner(m, cs, e)
         return remote(
-            ysend.at[zs, e], ybuf.at[k, y, e], y_ssem.at[zs, e], y_rsem.at[k, y, e], at(z, h, c, lx, to)
+            ysend.at[zs, e, cs], ybuf.at[t, e, y], y_ssem.at[zs, e, cs], y_rsem.at[t, e, y],
+            at(z, h, c, lx, to),
         )
 
     def score(m, e, fresh):
@@ -205,111 +227,183 @@
                 handed(zs, s).wait_recv()
         lhs = qbuf[zs].reshape(96, half)
         part = lax.dot_general(lhs, tbuf[e], (((1,), (1,)), ((), ())), preferred_element_type=F32)
-        k = zs % 2 + 2 * (zs // 8)
-
-        @pl.when((zs // 2) % 4 == y)
+        for cs in (0, 1):
+            rows = part[48 * cs : 48 * cs + 48]
+
+            @pl.when(owner(m, cs, e) == y)
+            def _():
+                own[(m + 1) // 2, e] = rows
+
+            @pl.when(owner(m, cs, e) != y)
+            def _():
+                ysend[zs, e, cs] = rows.astype(BF16)
+                y_copy(m, cs, e).start()
+
+    def x_copy(m, e, col):
+        t = (m + 1) // 2
+        return remote(
+            xsend.at[t, e, col], xbuf.at[t, x], x_ssem.at[t, e, col], x_rsem.at[t, x], at_x(2 * e + col)
+        )
+
+    def f_copy(m):
+        zs, t = chunk(m), (m + 1) // 2
+        return remote(
+            fsend.at[t], fbuf.at[zs % 2, y % 2, lx], f_ssem.at[t], f_rsem.at[zs % 2, y % 2, lx],
+            at(z, h, c, zs // 8, (zs // 2) % 4),
+        )
+
+    def join(m, e):
+        zs, t = chunk(m), (m + 1) // 2
+
+        @pl.when(owner(m, y % 2, e) == y)
         def _():
-            own[k, e] = part
-
-        @pl.when((zs // 2) % 4 != y)
-        def _():
-            ysend[zs, e] = part.astype(BF16)
-            y_copy(zs, e).start()
-
-    def x_copy(zs, e):
-        k = zs % 2 + 2 * (zs // 8)
-        return remote(
-            xsend.at[k, e], xbuf.at[zs % 2, x], x_ssem.at[k, e], x_rsem.at[zs % 2, x],
-            at(z, e, c, zs // 8, y),
-        )
-
-    def join(m, e):
-        zs = chunk(m)
-        k = zs % 2 + 2 * (zs // 8)
-
-        @pl.when((zs // 2) % 4 == y)
-        def _():
-            total = own[k, e]
+            total = own[t, e]
             for step in (1, 2, 3):
                 src = (y + step) % 4
-                slot = ybuf.at[k, src, e]
-                remote(slot, slot, y_ssem.at[zs, e], y_rsem.at[k, src, e], right).wait_recv()
-                total = total + ybuf[k, src, e].astype(F32)
-            mine = 2 * e + zs // 8 == x
-
-            @pl.when(mine)
+                slot = ybuf.at[t, e, src]
+                remote(slot, slot, y_ssem.at[zs, e, 0], y_rsem.at[t, e, src], right).wait_recv()
+                total = total + ybuf[t, e, src].astype(F32)
+            for col in (0, 1):
+                part = total[:, 128 * col : 128 * col + 128].astype(xsend.dtype)
+
+                @pl.when(2 * e + col == x)
+                def _():
+                    xbuf[t, x] = part
+
+                @pl.when(2 * e + col != x)
+                def _():
+                    xsend[t, e, col] = part
+                    x_copy(m, e, col).start()
+
+    def kept(m):
+        zs = chunk(m)
+        return ((zs // 2) % 4 == y) & (zs // 8 == lx)
+
+    def finish(m):
+        zs, t = chunk(m), (m + 1) // 2
+
+        @pl.when(owner(m, y % 2, h) == y)
+        def _():
+            total = xbuf[t, x].astype(F32)
+            for step in (1, 2, 3):
+                src = (x + step) % 4
+                slot = xbuf.at[t, src]
+                remote(slot, slot, x_ssem.at[t, 0, 0], x_rsem.at[t, src], right).wait_recv()
+                total = total + xbuf[t, src].astype(F32)
+
+            @pl.when(kept(m))
             def _():
-                xbuf[zs % 2, x] = total
-
-            @pl.when(jnp.logical_not(mine))
+                fbuf[zs % 2, y % 2, lx] = total
+
+            @pl.when(jnp.logical_not(kept(m)))
             def _():
-                xsend[k, e] = total
-                x_copy(zs, e).start()
+                fsend[t] = total
+                f_copy(m).start()
 
     def over(lo, hi, f):
+        for edge in (0, 15):
+            if lo <= edge < hi:
+                f(edge)
+        lo, hi = max(lo, 1), min(hi, 15)
         if hi > lo:
 
             @pl.loop(lo, hi)
             def _(m):
                 f(m)
 
-    waiting = []
+    def pass_on(t, s):
+        for way in (0, 1):
+            zs = (z + 16 - t) % 16 if way == 0 else (z + t) % 16
+            ring(zs, s, way, t).wait_recv()
+            if t < 7 or (way == 0 and s == 0) or (way == 1 and s == 2):
+                ring(zs, s, way, t).start()
+            elif s == 1:
+
+                @pl.when(c == way)
+                def _():
+                    ring(zs, s, way, t).start()
+
+            hand(zs, s).start()
+
+    def mine(lo, hi):
+        over(lo, hi, lambda m: score(m, h, True))
+
+    def theirs(lo, hi):
+        over(lo, hi, lambda m: score(m, 1 - h, False))
+
+    def joins(items):
+        for lo, hi, e in items:
+            over(lo, hi, lambda m: join(m, e))
+
+    def finishes(items):
+        for lo, hi, e in items:
+            if e is not h:
+                over(lo, hi, finish)
+
+    scored, joined = [], []
     caught = 0
-    for t in range(1, 9):
-        for s in range(STEPS):
-            if t < 8:
-                for way in (0, 1):
-                    zs = (z + 16 - t) % 16 if way == 0 else (z + t) % 16
-                    ring(zs, s, way, t).wait_recv()
-                    if t < 7 or (way == 0 and s == 0) or (way == 1 and s == 2):
-                        ring(zs, s, way, t).start()
-                    elif s == 1:
-
-                        @pl.when(c == way)
-                        def _():
-                            ring(zs, s, way, t).start()
-
-                    hand(zs, s).start()
-            else:
-                zs = (z + 8) % 16
-                ring(zs, s, 0, 0).wait_recv()
-                hand(zs, s).start()
+    not_h = 1 - h
+
+    def settle(t):
+        while scored and scored[0][0] + LAG_Y <= t:
+            _, lo, hi, e = scored.pop(0)
+            joins([(lo, hi, e)])
+            joined.append((t, lo, hi, e))
+        while joined and joined[0][0] + LAG_X <= t:
+            finishes([joined.pop(0)[1:]])
+
+    for t in range(1, 8):
+        pass_on(t, 0)
         if t == 1:
             local_train.wait()
+        settle(t)
+        pass_on(t, 1)
         lo, hi = max(2 * t - 3, 0), 2 * t - 1
-        over(lo, hi, lambda m: score(m, h, True))
-        done = [(lo, hi, True)]
+        mine(lo, hi)
+        scored.append((t, lo, hi, h))
+        pass_on(t, 2)
         if t >= LATE:
             if t == LATE:
                 local = tbuf.at[1 - h]
                 remote(local, local, train_sem.at[1], train_sem.at[2], partner).wait_recv()
             top = min(caught + CATCH, hi)
-            over(caught, top, lambda m: score(m, 1 - h, False))
-            done.append((caught, top, False))
+            theirs(caught, top)
+            scored.append((t, caught, top, not_h))
             caught = top
-        for lo, hi, mine in waiting:
-            over(lo, hi, lambda m: join(m, h if mine else 1 - h))
-        waiting = done
-    score(15, h, True)
-    score(15, 1 - h, False)
-    for lo, hi, mine in waiting + [(15, 16, True), (15, 16, False)]:
-        over(lo, hi, lambda m: join(m, h if mine else 1 - h))
+    mine(13, 15)
+    theirs(caught, 15)
+    for s in range(STEPS):
+        ring((z + 8) % 16, s, 0, 0).wait_recv()
+        hand((z + 8) % 16, s).start()
+    settle(7 + LAG_Y - 1)
+    mine(15, 16)
+    theirs(15, 16)
+    settle(7 + LAG_Y)
+    joins([(13, 15, h), (caught, 15, not_h)])
+    finishes([item[1:] for item in joined])
+    joins([(15, 16, h), (15, 16, not_h)])
+    finishes([(caught, 15, not_h)])
+    finishes([(15, 16, not_h)])
 
     factor = 1.0 / math.sqrt(8 * 4096)
     for j in (0, 1):
-        total = xbuf[j, x]
-        for step in (1, 2, 3):
-            src = (x + step) % 4
-            slot = xbuf.at[j, src]
-            remote(slot, slot, x_ssem.at[0, 0], x_rsem.at[j, src], right).wait_recv()
-            total = total + xbuf[j, src]
-        total = total * factor
-        for cc in range(2):
-            for s in range(STEPS):
-                for hh in range(2):
-                    row = cc * 48 + s * 16 + hh * 8
-                    to = 32 * j + 16 * hh + 8 * cc
-                    out_ref[s, to : to + 8, :] = total[row : row + 8]
+        ahead = (2 * layer + j - z + 16) % 16
+        edge = (ahead == 0) | (ahead == 8)
+        group = jnp.where(edge, h, jnp.where(ahead > 8, 1, 0))
+        for cs in (0, 1):
+            for col in (0, 1):
+                slot = fbuf.at[j, cs, col]
+
+                @pl.when((2 * group + cs != y) | (col != lx))
+                def _():
+                    remote(slot, slot, f_ssem.at[0], f_rsem.at[j, cs, col], right).wait_recv()
+
+                total = fbuf[j, cs, col] * factor
+                for s in range(STEPS):
+                    for hh in range(2):
+                        to = 32 * j + 16 * hh + 8 * cs
+                        row = 16 * s + 8 * hh
+                        out_ref[s, to : to + 8, 128 * col : 128 * col + 128] = total[row : row + 8]
 
     send_train.wait_send()
     for s in range(STEPS):
@@ -329,48 +423,62 @@
     def _(zs):
         for s in range(STEPS):
             hand(zs, s).wait_send()
+
+    def sent(m):
         for e in (0, 1):
-
-            @pl.when((zs // 2) % 4 != y)
-            def _():
-                y_copy(zs, e).wait_send()
-
-            @pl.when(((zs // 2) % 4 == y) & (2 * e + zs // 8 != x))
-            def _():
-                x_copy(zs, e).wait_send()
+            for cs in (0, 1):
+
+                @pl.when(owner(m, cs, e) != y)
+                def _():
+                    y_copy(m, cs, e).wait_send()
+
+            for col in (0, 1):
+
+                @pl.when((owner(m, y % 2, e) == y) & (2 * e + col != x))
+                def _():
+                    x_copy(m, e, col).wait_send()
+
+        @pl.when((owner(m, y % 2, h) == y) & jnp.logical_not(kept(m)))
+        def _():
+            f_copy(m).wait_send()
+
+    over(0, 16, sent)
 
 
 def body(train_grads, query_grads, out_basis, in_basis, eigenvalues, block_order):
     train = train_grads.reshape(256, 4096)
     query = query_grads.reshape(4, 8, 4096)
-    vmem = pl.BlockSpec(memory_space=pltpu.VMEM)
     dma = pltpu.SemaphoreType.DMA
     return pl.pallas_call(
         kernel,
         out_shape=jax.ShapeDtypeStruct((STEPS, 64, 256), F32),
-        in_specs=[
-            pl.BlockSpec(memory_space=pltpu.SMEM),
-            pl.BlockSpec(memory_space=pl.ANY),
-            vmem, vmem, vmem, vmem,
-        ],
-        out_specs=vmem,
+        in_specs=[pl.BlockSpec(memory_space=pltpu.HBM)] * 6,
+        out_specs=pl.BlockSpec(memory_space=pltpu.VMEM),
         scratch_shapes=[
+            pltpu.SMEM((4,), jnp.int32),
+            pltpu.VMEM((4, 8, 4096), BF16),
+            pltpu.VMEM((1, 64, 64), F32),
+            pltpu.VMEM((1, 64, 64), F32),
+            pltpu.VMEM((1, 4096), F32),
+            dma((5,)),
             pltpu.VMEM((2, 256, 2048), BF16),
             pltpu.VMEM((16, 2, 3, 16, 2048), BF16),
             pltpu.VMEM((3, 2, 128, 128), F32),
             pltpu.VMEM((3, 16, 1024), BF16),
             pltpu.VMEM((3, 16, 1024), BF16),
-            pltpu.VMEM((4, 2, 96, 256), F32),
-            pltpu.VMEM((16, 2, 96, 256), BF16),
-            pltpu.VMEM((4, 4, 2, 96, 256), BF16),
-            pltpu.VMEM((4, 2, 96, 256), F32),
-            pltpu.VMEM((2, 4, 96, 256), F32),
+            pltpu.VMEM((9, 2, 48, 256), F32),
+            pltpu.VMEM((16, 2, 2, 48, 256), BF16),
+            pltpu.VMEM((9, 2, 4, 48, 256), BF16),
+            pltpu.VMEM((9, 2, 2, 48, 128), F32),
+            pltpu.VMEM((9, 4, 48, 128), F32),
+            pltpu.VMEM((9, 48, 128), F32),
+            pltpu.VMEM((2, 2, 2, 48, 128), F32),
             dma((3,)), dma((3,)), dma((3,)),
             dma((2, 8, 3)), dma((16, 3)), dma((16, 3)), dma((16, 3)),
-            dma((16, 2)), dma((4, 4, 2)), dma((4, 2)), dma((2, 4)),
+            dma((16, 2, 2)), dma((9, 2, 4)), dma((9, 2, 2)), dma((9, 4)), dma((9,)), dma((2, 2, 2)),
         ],
         compiler_params=pltpu.CompilerParams(
-            collective_id=0, has_side_effects=True, vmem_limit_bytes=48 << 20
+            collective_id=0, has_side_effects=True, vmem_limit_bytes=63 << 20
         ),
     )(block_order, train, query, out_basis, in_basis, eigenvalues)
 

time: 84.4 us -> 77.7 us (0.921)
  the two profiles are of different devices: /device:TPU:38 before, /device:TPU:6 now
where the time goes in v2:
time: 77.7 us; the launch traced here: 77.5 us
  Pallas kernels  75.9 us (98%)
  local copies, waits for them, and re-layouts  1.62 us (2%)
    pallas_call x1, Pallas kernels, body(): pl.pallas_call(kernel, out_shape=jax.ShapeDtypeStruct((STEPS, 64, 256), F...  75.9 us
    unnamed x1, local copies, waits for them, and re-layouts  1.62 us

profile of v2, /device:TPU:6, one launch (start us, length us, event | category | flops | bytes accessed | tf_op | source)
XLA Modules:
  0.0 77.5 jit_solution(17444830166389452643)
XLA Ops:
  0.0 75.9 %shard_map.64 = f32[3,64,256]{2,1,0:T(8,128)} custom-call(s32[4]{0:T(128)} %order_hbm.1, bf16[256,4096]{1,0:T(8,128)(2,1)} %bitcast.2, bf16[4,8,4096]{2,1,0:T(8,128)(2,1)} %bitcast.3, f32[1,64,64]{2,1,0:T(8,128)} %a_hbm.1, f32[1,64,64]{2,1,0:T(8,128)} %b_hbm.1, f32[1,4096]{1,0:T(1,128)} %lam_hbm.1), custom_call_target="tpu_custom_call" | custom-call | tf_op jit(solution)/shard_map/pallas_call | solution.py:452
  75.9 1.6 %copy.8 = f32[3,64,256]{2,1,0:T(8,128)} copy(f32[3,64,256]{2,1,0:T(8,128)} %shard_map.64) | data formatting | bytes 393216

commit v3 on v2

v3 whole, which is shorter than its diff:
```python
import math

import jax
import jax.numpy as jnp
from jax import lax
from jax.experimental import pallas as pl
from jax.experimental.pallas import tpu as pltpu
from jax.sharding import PartitionSpec as P

STEPS = 3
MESH = pl.DeviceIdType.MESH
F32 = jnp.float32
BF16 = jnp.bfloat16
EDGES = (0, 32, 256)
LAG_Y = 2
LAG_X = 2
LATE = 5
CATCH = 3


def mm(a, b):
    return lax.dot_general(a, b, (((1,), (0,)), ((), ())), preferred_element_type=F32)


def split(x, parts):
    out = []
    for _ in range(parts):
        top = x.astype(BF16)
        out.append(top)
        x = x - top.astype(F32)
    return out


def mm3(x, y):
    return mm(x[0], y[0]) + (mm(x[0], y[1]) + mm(x[1], y[0]))


def twice(m):
    zero = jnp.zeros_like(m)
    return jnp.concatenate(
        [jnp.concatenate([m, zero], axis=1), jnp.concatenate([zero, m], axis=1)], axis=0
    )


def patterns():
    rows = lax.broadcasted_iota(jnp.int32, (512, 64), 0)
    cols = lax.broadcasted_iota(jnp.int32, (512, 64), 1)
    pick_row = ((rows >> 8) + 2 * ((rows & 255) >> 3) == cols).astype(F32).astype(BF16)
    k_rows = lax.broadcasted_iota(jnp.int32, (64, 512), 0)
    k_cols = lax.broadcasted_iota(jnp.int32, (64, 512), 1)
    pick_col = ((k_cols >> 8) + 2 * ((k_cols & 255) >> 3) == k_rows).astype(F32).astype(BF16)
    row_q = lax.broadcasted_iota(jnp.int32, (512, 512), 0) & 7
    col_q = lax.broadcasted_iota(jnp.int32, (512, 512), 1) & 7
    return pick_row, pick_col, row_q == col_q


def spread(m_parts, pick_row, pick_col, same):
    out = []
    for part in m_parts:
        tall = mm(pick_row, part).astype(BF16)
        full = mm(tall, pick_col)
        out.append(jnp.where(same, full, 0.0).astype(BF16))
    return out


def left_apply(kron_parts, blocks):
    lane = lax.broadcasted_iota(jnp.int32, (256, 128), 1)
    low = lane < 64

    def turn(v):
        return pltpu.roll(v, 64, 1)

    b0, b1, b2 = blocks
    even = jnp.concatenate([jnp.where(low, b0, turn(b1)), b2], axis=1)
    odd = jnp.concatenate([jnp.where(low, turn(b0), b1), turn(b2)], axis=1)
    right = jnp.concatenate([even, odd], axis=0)
    out = mm3(kron_parts, split(right, 2))
    top, bot = out[:256], out[256:]
    r0 = jnp.where(low, top[:, :128], turn(bot[:, :128]))
    r1 = jnp.where(low, turn(top[:, :128]), bot[:, :128])
    r2 = jnp.where(low, top[:, 128:], turn(bot[:, 128:]))
    return r0, r1, r2


def stack_groups(x, count):
    return jnp.concatenate([x[:, g * 128 : (g + 1) * 128] for g in range(count)], axis=0)


def unstack_groups(x, first, count):
    return jnp.concatenate([x[(first + g) * 8 : (first + g + 1) * 8] for g in range(count)], axis=1)


def kernel(
    order_hbm, train_ref, query_hbm, a_hbm, b_hbm, lam_hbm, out_ref,
    order_ref, query_ref, a_ref, b_ref, lam_ref, in_sem, tbuf, qbuf, pf, xqs, own, ysend, ybuf, xsend, xbuf, fsend, fbuf,
    train_sem, train_ssem, train_rsem, xq_ssem, xq_rsem, zs_ssem, c_ssem, z_rsem, c_rsem, y_ssem, y_rsem, x_ssem, x_rsem, f_ssem, f_rsem,
):
    dp = lax.axis_index("dp")
    layer = lax.axis_index("layer")
    z, h, c = dp // 4, (dp // 2) % 2, dp % 2
    lx, y = layer // 4, layer % 4
    x = 2 * h + lx

    def at(zz, hh, cc, ll, yy):
        return (4 * zz + 2 * hh + cc, 4 * ll + yy)

    copies = [
        pltpu.make_async_copy(src, dst, in_sem.at[i])
        for i, (src, dst) in enumerate(
            [
                (a_hbm, a_ref), (b_hbm, b_ref), (query_hbm, query_ref),
                (order_hbm, order_ref), (lam_hbm, lam_ref),
            ]
        )
    ]
    for copy in copies:
        copy.start()

    def at_x(xx):
        return at(z, xx // 2, c, xx % 2, y)

    right, left = at((z + 1) % 16, h, c, lx, y), at((z + 15) % 16, h, c, lx, y)
    other_core = at(z, h, 1 - c, lx, y)
    partner = at(z, 1 - h, c, lx, y)

    barrier = pltpu.get_barrier_semaphore()
    everyone = [right, left, other_core]
    for step in (1, 2, 3):
        aside = (y + step) % 4
        everyone += [at(z, h, c, lx, aside), at(z, h, c, 1 - lx, aside), at_x((x + step) % 4)]
    for device in everyone:
        pl.semaphore_signal(barrier, inc=1, device_id=device, device_id_type=MESH)

    def remote(src, dst, ssem, rsem, device):
        return pltpu.make_async_remote_copy(
            src_ref=src, dst_ref=dst, send_sem=ssem, recv_sem=rsem, device_id=device, device_id_type=MESH
        )

    half = 2048
    local_train = pltpu.make_async_copy(
        train_ref.at[:, pl.ds(pl.multiple_of(h * half, half), half)], tbuf.at[h], train_sem
    )
    local_train.start()

    def train_copy(piece):
        rows = pl.ds(EDGES[piece], EDGES[piece + 1] - EDGES[piece])
        return remote(
            train_ref.at[rows, pl.ds(pl.multiple_of((1 - h) * half, half), half)],
            tbuf.at[h, rows], train_ssem.at[piece], train_rsem.at[piece], partner,
        )

    shapes = patterns()
    copies[0].wait()
    copies[1].wait()
    b_mat = b_ref[0]
    a_mat = a_ref[0]
    forth = split(twice(b_mat), 3)
    back = split(twice(b_mat.T), 2)
    a_parts = split(a_mat, 2)
    at_parts = split(a_mat.T, 2)
    kron_in = spread(at_parts, *shapes)
    kron_out = spread(a_parts, *shapes)
    for copy in copies[2:]:
        copy.wait()
    pl.semaphore_wait(barrier, len(everyone))
    train_copy(0).start()
    lam = lam_ref[...]
    lam_rows = jnp.concatenate(
        [jnp.broadcast_to(lam[:, g * 128 : (g + 1) * 128], (8, 128)) for g in range(32)], axis=0
    )
    first = []
    for s in range(STEPS):
        raw = stack_groups(query_ref[order_ref[s]].astype(F32), 32).astype(BF16)
        first.append(mm(raw, forth[0]) + (mm(raw, forth[1]) + mm(raw, forth[2])))
    rotated = left_apply(kron_in, first)
    scaled = [mm3(split(r / lam_rows, 2), back) for r in rotated]
    ready = left_apply(kron_out, scaled)
    for s in range(STEPS):
        pf[s, 0] = ready[s][:128]
        pf[s, 1] = ready[s][128:]


    def unit(zs, cc, u):
        hh = h if u < 2 else 1 - h
        return qbuf.at[zs, cc, hh, pl.ds(0, 32) if u % 2 == 0 else pl.ds(32, 16)]

    def ring(zs, u, way, t):
        slot = unit(zs, c, u)
        return remote(slot, slot, zs_ssem.at[way, t, u], z_rsem.at[zs, u], right if way == 0 else left)

    def hand(zs, u):
        slot = unit(zs, c, u)
        return remote(slot, slot, c_ssem.at[zs, u], c_rsem.at[zs, u], other_core)

    def handed(zs, u):
        slot = unit(zs, 1 - c, u)
        return remote(slot, slot, c_ssem.at[zs, u], c_rsem.at[zs, u], other_core)

    def xq(u):
        rows = pl.ds(0, 32) if u == 0 else pl.ds(32, 16)
        return remote(xqs.at[rows], qbuf.at[z, c, h, rows], xq_ssem.at[u], xq_rsem.at[u], partner)

    def xq_in(u):
        slot = unit(z, c, 2 + u)
        return remote(slot, slot, xq_ssem.at[u], xq_rsem.at[u], partner)

    def tall(part):
        return jnp.concatenate([unstack_groups(part, 0, 8), unstack_groups(part, 8, 8)], axis=0)

    def launch(u):
        ring(z, u, 0, 0).start()
        ring(z, u, 1, 0).start()
        hand(z, u).start()

    xqs[...] = jnp.concatenate([tall(pf[s, 1 - h]) for s in range(STEPS)], axis=0).astype(BF16)
    xq(0).start()
    xq(1).start()
    qbuf[z, c, h] = jnp.concatenate([tall(pf[s, h]) for s in range(STEPS)], axis=0).astype(BF16)
    launch(0)
    launch(1)
    train_copy(1).start()
    for u in (0, 1):
        xq_in(u).wait_recv()
        launch(2 + u)

    def lone(d):
        return isinstance(d, int) and d in (0, 8)

    def chunks(d):
        return [(z + d) % 16] if lone(d) else [(z + 16 - d) % 16, (z + d) % 16]

    def my_chunk(d):
        return (z + d) % 16 if lone(d) else (z + 16 + (1 - 2 * (y // 2)) * d) % 16

    def y_copy(d, e, to):
        return remote(
            ysend.at[d, e, to], ybuf.at[d, e, y], y_ssem.at[d, e, to], y_rsem.at[d, e, y],
            at(z, h, c, lx, to),
        )

    def wide(zs):
        rows = qbuf[zs].astype(F32).reshape(12, 16, 1024)
        low, high = rows[:, :8].reshape(96, 1024), rows[:, 8:].reshape(96, 1024)
        return jnp.concatenate([low, high], axis=1).astype(BF16)

    def score(d, e, fresh):
        held = chunks(d)
        if fresh:
            for zs in held:
                for u in range(4):
                    handed(zs, u).wait_recv()
        lhs = jnp.concatenate([wide(zs) for zs in held], axis=0)
        part = lax.dot_general(lhs, tbuf[e], (((1,), (1,)), ((), ())), preferred_element_type=F32)
        for piece in range(2 * len(held)):
            rows = part[48 * piece : 48 * piece + 48]
            to = 2 * e + piece if lone(d) else (2, 3, 0, 1)[piece]

            @pl.when(to == y)
            def _():
                own[d, e] = rows

            ysend[d, e, to] = rows.astype(BF16)
        for step in (1, 2, 3):
            to = (y + step) % 4
            if lone(d):

                @pl.when(to // 2 == e)
                def _():
                    y_copy(d, e, to).start()

            else:
                y_copy(d, e, to).start()

    def x_copy(d, e, col):
        return remote(
            xsend.at[d, e, col], xbuf.at[d, x], x_ssem.at[d, e, col], x_rsem.at[d, x], at_x(2 * e + col)
        )

    def f_copy(d):
        zs = my_chunk(d)
        return remote(
            fsend.at[d], fbuf.at[zs % 2, y % 2, lx], f_ssem.at[d], f_rsem.at[zs % 2, y % 2, lx],
            at(z, h, c, zs // 8, (zs // 2) % 4),
        )

    def guarded(d, e, f):
        if lone(d):
            pl.when(y // 2 == e)(f)
        else:
            f()

    def join(d, e):
        for step in (1, 2, 3):
            to = (y + step) % 4
            if lone(d):

                @pl.when(to // 2 == e)
                def _():
                    y_copy(d, e, to).wait_send()

            else:
                y_copy(d, e, to).wait_send()

        def run():
            total = own[d, e]
            for step in (1, 2, 3):
                src = (y + step) % 4
                slot = ybuf.at[d, e, src]
                remote(slot, slot, y_ssem.at[d, e, 0], y_rsem.at[d, e, src], right).wait_recv()
                total = total + ybuf[d, e, src].astype(F32)
            for col in (0, 1):
                part = total[:, 128 * col : 128 * col + 128].astype(xsend.dtype)

                @pl.when(2 * e + col == x)
                def _():
                    xbuf[d, x] = part

                @pl.when(2 * e + col != x)
                def _():
                    xsend[d, e, col] = part
                    x_copy(d, e, col).start()

        guarded(d, e, run)

    def kept(d):
        zs = my_chunk(d)
        return ((zs // 2) % 4 == y) & (zs // 8 == lx)

    def finish(d):
        def run():
            zs = my_chunk(d)
            total = xbuf[d, x].astype(F32)
            for step in (1, 2, 3):
                src = (x + step) % 4
                slot = xbuf.at[d, src]
                remote(slot, slot, x_ssem.at[d, 0, 0], x_rsem.at[d, src], right).wait_recv()
                total = total + xbuf[d, src].astype(F32)

            @pl.when(kept(d))
            def _():
                fbuf[zs % 2, y % 2, lx] = total

            @pl.when(jnp.logical_not(kept(d)))
            def _():
                fsend[d] = total
                f_copy(d).start()

        guarded(d, h, run)

    def over(lo, hi, f):
        for edge in (0, 8):
            if lo <= edge < hi:
                f(edge)
        lo, hi = max(lo, 1), min(hi, 8)
        if hi == lo + 1:
            f(lo)
        elif hi > lo:

            @pl.loop(lo, hi)
            def _(d):
                f(d)

    def pass_on(t, u):
        for way in (0, 1):
            zs = (z + 16 - t) % 16 if way == 0 else (z + t) % 16
            ring(zs, u, way, t).wait_recv()
            if t < 7 or way == u // 2:
                ring(zs, u, way, t).start()
            hand(zs, u).start()

    def sent_on(t):
        for way in (0, 1) if 0 < t < 8 else (0,):
            zs = (z + 16 - t) % 16 if way == 0 else (z + t) % 16
            for u in range(4):
                hand(zs, u).wait_send()
                if t == 0:
                    ring(zs, u, 0, t).wait_send()
                    ring(zs, u, 1, t).wait_send()
                elif t < 7 or (t == 7 and way == u // 2):
                    ring(zs, u, way, t).wait_send()

    def joins(lo, hi, e):
        over(lo, hi, lambda d: join(d, e))

    def finishes(lo, hi, e):
        if e is not h:
            over(lo, hi, finish)

    scored, joined = [], []
    caught = 0
    not_h = 1 - h

    def settle(t):
        while scored and scored[0][0] + LAG_Y <= t:
            _, lo, hi, e = scored.pop(0)
            joins(lo, hi, e)
            joined.append((t, lo, hi, e))
        while joined and joined[0][0] + LAG_X <= t:
            finishes(*joined.pop(0)[1:])

    def mine(t, d):
        score(d, h, True)
        scored.append((t, d, d + 1, h))

    def theirs(t, lo, hi):
        over(lo, hi, lambda d: score(d, not_h, False))
        scored.append((t, lo, hi, not_h))

    for t in range(1, 8):
        pass_on(t, 0)
        if t == 1:
            local_train.wait()
        settle(t)
        pass_on(t, 1)
        mine(t, t - 1)
        pass_on(t, 2)
        pass_on(t, 3)
        if t >= 2:
            sent_on(t - 2)
        if t >= LATE:
            if t == LATE:
                for piece in (0, 1):
                    rows = pl.ds(EDGES[piece], EDGES[piece + 1] - EDGES[piece])
                    local = tbuf.at[1 - h, rows]
                    remote(local, local, train_ssem.at[0], train_rsem.at[piece], partner).wait_recv()
            top = min(caught + CATCH, t)
            theirs(t, caught, top)
            caught = top
    mine(8, 7)
    theirs(8, caught, 8)
    for u in range(4):
        ring((z + 8) % 16, u, 0, 0).wait_recv()
        hand((z + 8) % 16, u).start()
    settle(6 + LAG_Y)
    mine(9, 8)
    theirs(9, 8, 9)
    settle(7 + LAG_Y)
    settle(8 + LAG_Y)
    settle(9 + LAG_Y)
    settle(99)

    factor = 1.0 / math.sqrt(8 * 4096)
    for j in (0, 1):
        ahead = (2 * layer + j - z + 16) % 16
        edge = (ahead == 0) | (ahead == 8)
        group = jnp.where(edge, h, jnp.where(ahead > 8, 1, 0))
        for cs in (0, 1):
            for col in (0, 1):
                slot = fbuf.at[j, cs, col]

                @pl.when((2 * group + cs != y) | (col != lx))
                def _():
                    remote(slot, slot, f_ssem.at[0], f_rsem.at[j, cs, col], right).wait_recv()

                total = fbuf[j, cs, col] * factor
                for s in range(STEPS):
                    for hh in range(2):
                        to = 32 * j + 16 * hh + 8 * cs
                        row = 24 * hh + 8 * s
                        out_ref[s, to : to + 8, 128 * col : 128 * col + 128] = total[row : row + 8]

    for piece in (0, 1):
        train_copy(piece).wait_send()
    for u in (0, 1):
        xq(u).wait_send()
    for t in (6, 7, 8):
        sent_on(t)

    def sent(d):
        for e in (0, 1):

            def run():
                for col in (0, 1):

                    @pl.when(2 * e + col != x)
                    def _():
                        x_copy(d, e, col).wait_send()

            guarded(d, e, run)

        def last():
            @pl.when(jnp.logical_not(kept(d)))
            def _():
                f_copy(d).wait_send()

        guarded(d, h, last)

    over(0, 9, sent)


def body(train_grads, query_grads, out_basis, in_basis, eigenvalues, block_order):
    train = train_grads.reshape(256, 4096)
    query = query_grads.reshape(4, 8, 4096)
    dma = pltpu.SemaphoreType.DMA
    return pl.pallas_call(
        kernel,
        out_shape=jax.ShapeDtypeStruct((STEPS, 64, 256), F32),
        in_specs=[pl.BlockSpec(memory_space=pltpu.HBM)] * 6,
        out_specs=pl.BlockSpec(memory_space=pltpu.VMEM),
        scratch_shapes=[
            pltpu.SMEM((4,), jnp.int32),
            pltpu.VMEM((4, 8, 4096), BF16),
            pltpu.VMEM((1, 64, 64), F32),
            pltpu.VMEM((1, 64, 64), F32),
            pltpu.VMEM((1, 4096), F32),
            dma((5,)),
            pltpu.VMEM((2, 256, 2048), BF16),
            pltpu.VMEM((16, 2, 2, 48, 1024), BF16),
            pltpu.VMEM((3, 2, 128, 128), F32),
            pltpu.VMEM((48, 1024), BF16),
            pltpu.VMEM((9, 2, 48, 256), F32),
            pltpu.VMEM((9, 2, 4, 48, 256), BF16),
            pltpu.VMEM((9, 2, 4, 48, 256), BF16),
            pltpu.VMEM((9, 2, 2, 48, 128), F32),
            pltpu.VMEM((9, 4, 48, 128), F32),
            pltpu.VMEM((9, 48, 128), F32),
            pltpu.VMEM((2, 2, 2, 48, 128), F32),
            dma, dma((2,)), dma((2,)), dma((2,)), dma((2,)),
            dma((2, 8, 4)), dma((16, 4)), dma((16, 4)), dma((16, 4)),
            dma((9, 2, 4)), dma((9, 2, 4)), dma((9, 2, 2)), dma((9, 4)), dma((9,)), dma((2, 2, 2)),
        ],
        compiler_params=pltpu.CompilerParams(
            collective_id=0, has_side_effects=True, vmem_limit_bytes=63 << 20
        ),
    )(block_order, train, query, out_basis, in_basis, eigenvalues)


def solution(mesh):
    placed = (
        P("dp", "layer", None),
        P(None, "dp", "layer", None),
        P("layer", None, None),
        P("layer", None, None),
        P("layer", None),
        P(),
    )
    return jax.shard_map(
        body, mesh=mesh, in_specs=placed, out_specs=P(None, "layer", "dp"), check_vma=False
    )
```

time: 77.7 us -> 74.9 us (0.964)
  Pallas kernels: 75.9 us -> 73.1 us
    pallas_call x1, Pallas kernels: 75.9 us -> 73.1 us  [body(): pl.pallas_call(kernel, out_shape=jax.ShapeDtypeStruct((STEPS, 64, 256), F...]
where the time goes in v3:
time: 74.9 us; the launch traced here: 74.7 us
  Pallas kernels  73.1 us (98%)
  local copies, waits for them, and re-layouts  1.62 us (2%)
    pallas_call x1, Pallas kernels, body(): pl.pallas_call(kernel, out_shape=jax.ShapeDtypeStruct((STEPS, 64, 256), F...  73.1 us
    unnamed x1, local copies, waits for them, and re-layouts  1.62 us

profile of v3, /device:TPU:6, one launch (start us, length us, event | category | flops | bytes accessed | tf_op | source)
XLA Modules:
  0.0 74.7 jit_solution(7952946860549901142)
XLA Ops:
  0.0 73.1 %shard_map.64 = f32[3,64,256]{2,1,0:T(8,128)} custom-call(s32[4]{0:T(128)} %order_hbm.1, bf16[256,4096]{1,0:T(8,128)(2,1)} %bitcast.2, bf16[4,8,4096]{2,1,0:T(8,128)(2,1)} %bitcast.3, f32[1,64,64]{2,1,0:T(8,128)} %a_hbm.1, f32[1,64,64]{2,1,0:T(8,128)} %b_hbm.1, f32[1,4096]{1,0:T(1,128)} %lam_hbm.1), custom_call_target="tpu_custom_call" | custom-call | tf_op jit(solution)/shard_map/pallas_call | solution.py:495
  73.1 1.6 %copy.8 = f32[3,64,256]{2,1,0:T(8,128)} copy(f32[3,64,256]{2,1,0:T(8,128)} %shard_map.64) | data formatting | bytes 393216

commit v4 on v3

--- a/solution.py
+++ b/solution.py
@@ -434,8 +434,6 @@
     settle(6 + LAG_Y)
     mine(9, 8)
     theirs(9, 8, 9)
-    settle(7 + LAG_Y)
-    settle(8 + LAG_Y)
     settle(9 + LAG_Y)
     settle(99)
 
@@ -511,8 +509,8 @@
             pltpu.VMEM((9, 2, 48, 256), F32),
             pltpu.VMEM((9, 2, 4, 48, 256), BF16),
             pltpu.VMEM((9, 2, 4, 48, 256), BF16),
-            pltpu.VMEM((9, 2, 2, 48, 128), F32),
-            pltpu.VMEM((9, 4, 48, 128), F32),
+            pltpu.VMEM((9, 2, 2, 48, 128), BF16),
+            pltpu.VMEM((9, 4, 48, 128), BF16),
             pltpu.VMEM((9, 48, 128), F32),
             pltpu.VMEM((2, 2, 2, 48, 128), F32),
             dma, dma((2,)), dma((2,)), dma((2,)), dma((2,)),

time: 74.9 us -> 73.7 us (0.984)
  Pallas kernels: 73.1 us -> 71.9 us
    pallas_call x1, Pallas kernels: 73.1 us -> 71.9 us  [body(): pl.pallas_call(kernel, out_shape=jax.ShapeDtypeStruct((STEPS, 64, 256), F...]
where the time goes in v4:
time: 73.7 us; the launch traced here: 73.5 us
  Pallas kernels  71.9 us (98%)
  local copies, waits for them, and re-layouts  1.62 us (2%)
    pallas_call x1, Pallas kernels, body(): pl.pallas_call(kernel, out_shape=jax.ShapeDtypeStruct((STEPS, 64, 256), F...  71.9 us
    unnamed x1, local copies, waits for them, and re-layouts  1.62 us

profile of v4, /device:TPU:6, one launch (start us, length us, event | category | flops | bytes accessed | tf_op | source)
XLA Modules:
  0.0 73.5 jit_solution(14186980803914372515)
XLA Ops:
  0.0 71.9 %shard_map.64 = f32[3,64,256]{2,1,0:T(8,128)} custom-call(s32[4]{0:T(128)} %order_hbm.1, bf16[256,4096]{1,0:T(8,128)(2,1)} %bitcast.2, bf16[4,8,4096]{2,1,0:T(8,128)(2,1)} %bitcast.3, f32[1,64,64]{2,1,0:T(8,128)} %a_hbm.1, f32[1,64,64]{2,1,0:T(8,128)} %b_hbm.1, f32[1,4096]{1,0:T(1,128)} %lam_hbm.1), custom_call_target="tpu_custom_call" | custom-call | tf_op jit(solution)/shard_map/pallas_call | solution.py:493
  71.9 1.6 %copy.8 = f32[3,64,256]{2,1,0:T(8,128)} copy(f32[3,64,256]{2,1,0:T(8,128)} %shard_map.64) | data formatting | bytes 393216
